TPU v7x, 256 devices: a whole 4x4x8 slice. The times are simulated.
256 devices in a mesh: ctx: 32 (over z_lo, x, core), tp: 8 (over z_hi, y).
Axes of the slice: x: 4, y: 4, z: 8 (z_hi: 2, z_lo: 4; z = z_hi * 4 + z_lo), core: 2. Of those that a mesh axis runs over, the one named last changes fastest.
Arguments:
- tokens: bfloat16 [16384, 8192], P('ctx', 'tp'), may hold values from -6 to 6
- in_weight: bfloat16 [8192, 3, 1024], P('tp'), may hold values from -0.0625 to 0.0625
- skip_gain: float32 [1024], P('tp'), may hold values from 0.5 to 1.5
- response: float32 [2, 512, 64, 1024], P(None, None, 'ctx', 'tp'), may hold values from -6 to 6
Outputs:
- mixed: bfloat16 [16384, 1024], P('ctx', 'tp')
All inputs are finite; a program needn't handle non-finite values.
Results may differ from a plain program's by a relative error of at most 0.027.
Values may be sent and summed in bfloat16 or wider, within the bound.
A program may use at most 64 MiB of HBM per device.

v0:
```python
import functools
import math

import jax
import jax.numpy as jnp
import numpy as np
from jax import lax
from jax.experimental import pallas as pl
from jax.experimental.pallas import tpu as pltpu
from jax.sharding import PartitionSpec as P

MESH = pl.DeviceIdType.MESH
F32 = jnp.float32
BF16 = jnp.bfloat16
UNITS = 6


def tables():
    row = np.arange(256)
    dev, inner = row // 8, row % 8
    rev = sum(((dev >> level) & 1) << (4 - level) for level in range(5))
    k1 = 2 * rev + inner % 2 + 64 * (inner // 2)
    col = np.arange(128)
    n1 = 4 * (col % 32) + col // 32
    n2 = np.arange(128)
    ang1 = 2 * np.pi / 256 * (k1[:, None] * n1[None, :] % 256)
    first = np.concatenate([np.cos(ang1), -np.sin(ang1)], axis=0)
    last = np.concatenate([np.cos(ang1).T, -np.sin(ang1).T], axis=1) / 32768
    ang2 = 2 * np.pi / 128 * (n2[:, None] * n2[None, :] % 128)
    c2, s2 = np.cos(ang2), np.sin(ang2)
    second = np.block([[c2, -s2], [s2, c2]])
    back = np.block([[c2, s2], [-s2, c2]])
    tw = 2 * np.pi / 32768 * (k1[:, None] * n2[None, :])
    bf = lambda a: jnp.asarray(a.astype(np.float32).astype(BF16))
    twist = jnp.asarray(np.stack([np.cos(tw), np.sin(tw)]).astype(np.float32))
    return bf(first), bf(second), bf(back), bf(last), twist


def kernel(tok_h, w_h, skip_ref, rsp_h, f1_h, f2_h, g2_h, g1_h, tw_h, o_ref,
           tok, w, rsp, f1, f2, g2, g1, tw,
           sa, ra, sb, rb, sc, rc, part, gat, query,
           hs32, hs, hr, g32, gs, gr, cs, cr,
           load_sem, sa_sem, ra_sem, sb_sem, rb_sem, sc_sem, rc_sem, x_send, x_recv):
    me = lax.axis_index("ctx")
    t = lax.axis_index("tp")
    zh, y = t // 4, t % 4
    up = (me, zh * 4 + (y + 1) % 4)
    down = (me, zh * 4 + (y + 3) % 4)
    across = (me, (1 - zh) * 4 + y)

    loads = [(tok_h, tok), (w_h.at[1], w.at[1]), (w_h.at[2], w.at[2]), (rsp_h, rsp), (w_h.at[0], w.at[0]),
             (f1_h, f1), (f2_h, f2), (g2_h, g2), (g1_h, g1), (tw_h, tw)]
    loads = [pltpu.make_async_copy(src, dst, load_sem.at[i]) for i, (src, dst) in enumerate(loads)]
    for copy in loads:
        copy.start()

    barrier = pltpu.get_barrier_semaphore()
    for dev in (up, down, across):
        pl.semaphore_signal(barrier, inc=1, device_id=dev, device_id_type=MESH)

    def greet(k, carry):
        pl.semaphore_signal(barrier, inc=1, device_id=((me + k) % 32, t), device_id_type=MESH)
        return carry

    lax.fori_loop(1, 32, greet, 0)

    def term(u, dest_y):
        rows = pl.ds(u % 2 * 256, 256)
        far = pl.ds(pl.multiple_of(((1 - zh) * 4 + dest_y) * 128, 128), 128)
        near = pl.ds(pl.multiple_of((zh * 4 + dest_y) * 128, 128), 128)
        if u < 2:
            rhs = [w[1, :, far], w[2, :, far]]
        elif u < 4:
            rhs = [w[1, :, near], w[2, :, near]]
        else:
            rhs = [w[0, :, far], w[0, :, near]]
        return jnp.dot(tok[rows, :], jnp.concatenate(rhs, axis=1), preferred_element_type=F32)

    def remote(src, dst, ssem, rsem, dev):
        return pltpu.make_async_remote_copy(src_ref=src, dst_ref=dst, send_sem=ssem, recv_sem=rsem,
                                            device_id=dev, device_id_type=MESH)

    lo, hi = pl.ds(0, 128), pl.ds(128, 128)

    def a_copy(u, side):
        part_rows = (lo, hi)[side]
        return remote(sa.at[u, part_rows], ra.at[u, part_rows], sa_sem.at[u, side], ra_sem.at[u, side], (up, down)[side])

    def b_copy(u, side, half):
        part_rows = (lo, hi)[half]
        return remote(sb.at[u, side, part_rows], rb.at[u, side, part_rows], sb_sem.at[u, 2 * side + half],
                      rb_sem.at[u, 2 * side + half], (up, down)[side])

    def c_copy(u):
        if u < 2:
            return remote(sc.at[u], rc.at[u], sc_sem.at[u], rc_sem.at[u], across)
        return remote(sc.at[u - 2, :, lo], rc.at[u - 2, :, lo], sc_sem.at[u - 2], rc_sem.at[u - 2], across)

    def compute_a(u):
        sa[u] = term(u, (y + 2) % 4).astype(BF16)

    def send_a(u):
        a_copy(u, 0).start()
        a_copy(u, 1).start()

    def raw(u):
        for side, step in ((0, 1), (1, 3)):
            value = term(u, (y + step) % 4)
            through, direct = (value[:128], value[128:]) if side == 0 else (value[128:], value[:128])
            sb[u, side, (hi, lo)[side], :] = direct.astype(BF16)
            b_copy(u, side, 1 - side).start()
            part[u % 2, side] = through

    def add(u):
        for side in (0, 1):
            a_copy(u, side).wait_recv()
            rows = (lo, hi)[side]
            sb[u, side, rows, :] = (part[u % 2, side] + ra[u, rows, :].astype(F32)).astype(BF16)
            b_copy(u, side, side).start()

    def finish(u):
        own = term(u, y)
        for side in (0, 1):
            for half in (0, 1):
                b_copy(u, side, half).wait_recv()
        total = own + rb[u, 0].astype(F32) + rb[u, 1].astype(F32)
        rows = pl.ds(u % 2 * 256, 256)
        if u < 2:
            sc[u] = total.astype(BF16)
            c_copy(u).start()
        elif u < 4:
            c_copy(u - 2).wait_recv()
            total = total + rc[u - 2].astype(F32)
            product = total[:, :128] * total[:, 128:]
            gat[rows, :] = product
            for half in (0, 1):
                s = u % 2 * 2 + half
                g32[pl.ds(s, 128, stride=4), :] = jnp.transpose(product[half * 128:half * 128 + 128, :])
        else:
            sc[u - 2, :, lo] = total[:, :128].astype(BF16)
            query[rows, :] = total[:, 128:]
            c_copy(u).start()

    def spread(src, dst, which):
        def go(k, carry):
            to = (me + k) % 32
            remote(src.at[to], dst.at[me], x_send.at[which], x_recv.at[which], (to, t)).start()
            return carry

        lax.fori_loop(1, 32, go, 0)
        dst[me] = src[me]

    def arrived(dst, which):
        others = dst.at[pl.ds(0, 31)]
        pltpu.make_async_copy(others, others, x_recv.at[which]).wait()

    def left(src, which):
        others = src.at[pl.ds(0, 31)]
        pltpu.make_async_copy(others, others, x_send.at[which]).wait()

    for i in range(3):
        loads[i].wait()
    compute_a(0)
    pl.semaphore_wait(barrier, 34)
    send_a(0)
    raw(0)
    compute_a(1)
    send_a(1)

    loads[3].wait()
    for ri in range(2):
        for b in range(8):
            hs32[pl.ds(ri * 8 + b, 128, stride=16), :] = jnp.transpose(rsp[ri, pl.ds(b, 128, stride=8), :])
    hs[...] = hs32[...].astype(BF16).reshape(32, 64, 128)
    spread(hs, hr, 0)

    add(0)
    raw(1)
    compute_a(2)
    send_a(2)
    add(1)
    finish(0)
    raw(2)
    compute_a(3)
    send_a(3)
    add(2)
    finish(1)
    raw(3)
    loads[4].wait()
    compute_a(4)
    send_a(4)
    add(3)
    finish(2)
    raw(4)
    finish(3)
    gs[...] = g32[...].astype(BF16).reshape(32, 16, 128)
    spread(gs, gr, 1)
    compute_a(5)
    send_a(5)
    add(4)
    raw(5)
    add(5)
    finish(4)
    for i in range(5, 10):
        loads[i].wait()
    arrived(hr, 0)
    arrived(gr, 1)

    g32[...] = gr[...].astype(F32).reshape(512, 128)
    signal = jnp.concatenate(
        [jnp.concatenate([g32[pl.ds(c * 4 + s, 32, stride=16), :] for s in range(4)], axis=0) for c in range(4)],
        axis=1).astype(BF16)
    mid = jnp.dot(f1[...], signal, preferred_element_type=F32)
    cosine, sine = tw[0], tw[1]
    columns = []
    for c in range(4):
        lanes = slice(c * 128, c * 128 + 128)
        re, im = mid[:256, lanes], mid[256:, lanes]
        turned = jnp.concatenate([re * cosine + im * sine, im * cosine - re * sine], axis=1).astype(BF16)
        spec = jnp.dot(turned, f2[...], preferred_element_type=F32)
        resp = hr[:, 16 * c:16 * c + 16, :].astype(F32)
        resp_re = resp[:, :8, :].reshape(256, 128)
        resp_im = resp[:, 8:, :].reshape(256, 128)
        re, im = spec[:, :128], spec[:, 128:]
        filtered = jnp.concatenate([re * resp_re - im * resp_im, re * resp_im + im * resp_re], axis=1).astype(BF16)
        back = jnp.dot(filtered, g2[...], preferred_element_type=F32)
        re, im = back[:, :128], back[:, 128:]
        columns.append(jnp.concatenate([re * cosine - im * sine, re * sine + im * cosine], axis=0).astype(BF16))
    conv = jnp.dot(g1[...], jnp.concatenate(columns, axis=1), preferred_element_type=F32)
    for c in range(4):
        for s in range(4):
            g32[pl.ds(c * 4 + s, 32, stride=16), :] = conv[s * 32:s * 32 + 32, c * 128:c * 128 + 128]
    cs[...] = g32[...].astype(BF16).reshape(32, 16, 128)
    spread(cs, cr, 2)

    finish(5)
    for u in (4, 5):
        c_copy(u).wait_recv()
    gain = skip_ref[...]
    arrived(cr, 2)
    g32[...] = cr[...].astype(F32).reshape(512, 128)
    for s in range(4):
        rows = pl.ds(s * 128, 128)
        conv_rows = jnp.transpose(g32[pl.ds(s, 128, stride=4), :])
        q = query[rows, :] + rc[2 + s // 2, pl.ds(s % 2 * 128, 128), lo].astype(F32)
        o_ref[rows, :] = (q * (conv_rows + gain * gat[rows, :])).astype(BF16)

    for u in range(UNITS):
        for side in (0, 1):
            a_copy(u, side).wait_send()
            for half in (0, 1):
                b_copy(u, side, half).wait_send()
    for u in (0, 1, 4, 5):
        c_copy(u).wait_send()
    for src, which in ((hs, 0), (gs, 1), (cs, 2)):
        left(src, which)


def per_device(tokens, in_weight, skip_gain, response):
    first, second, back, last, twist = tables()
    anywhere = pl.BlockSpec(memory_space=pltpu.HBM)
    vmem = pl.BlockSpec(memory_space=pltpu.VMEM)
    return pl.pallas_call(
        kernel,
        out_shape=jax.ShapeDtypeStruct((512, 128), BF16),
        in_specs=[anywhere, anywhere, vmem] + [anywhere] * 6,
        out_specs=vmem,
        scratch_shapes=[
            pltpu.VMEM((512, 1024), BF16),
            pltpu.VMEM((3, 1024, 1024), BF16),
            pltpu.VMEM((2, 1024, 128), F32),
            pltpu.VMEM((512, 128), BF16),
            pltpu.VMEM((256, 256), BF16),
            pltpu.VMEM((256, 256), BF16),
            pltpu.VMEM((128, 512), BF16),
            pltpu.VMEM((2, 256, 128), F32),
            pltpu.VMEM((UNITS, 256, 256), BF16),
            pltpu.VMEM((UNITS, 256, 256), BF16),
            pltpu.VMEM((UNITS, 2, 256, 256), BF16),
            pltpu.VMEM((UNITS, 2, 256, 256), BF16),
            pltpu.VMEM((4, 256, 256), BF16),
            pltpu.VMEM((4, 256, 256), BF16),
            pltpu.VMEM((2, 2, 128, 256), F32),
            pltpu.VMEM((512, 128), F32),
            pltpu.VMEM((512, 128), F32),
            pltpu.VMEM((2048, 128), F32),
            pltpu.VMEM((32, 64, 128), BF16),
            pltpu.VMEM((32, 64, 128), BF16),
            pltpu.VMEM((512, 128), F32),
            pltpu.VMEM((32, 16, 128), BF16),
            pltpu.VMEM((32, 16, 128), BF16),
            pltpu.VMEM((32, 16, 128), BF16),
            pltpu.VMEM((32, 16, 128), BF16),
            pltpu.SemaphoreType.DMA((10,)),
            pltpu.SemaphoreType.DMA((UNITS, 2)),
            pltpu.SemaphoreType.DMA((UNITS, 2)),
            pltpu.SemaphoreType.DMA((UNITS, 4)),
            pltpu.SemaphoreType.DMA((UNITS, 4)),
            pltpu.SemaphoreType.DMA((4,)),
            pltpu.SemaphoreType.DMA((4,)),
            pltpu.SemaphoreType.DMA((3,)),
            pltpu.SemaphoreType.DMA((3,)),
        ],
        compiler_params=pltpu.CompilerParams(
            collective_id=0, has_side_effects=True, vmem_limit_bytes=48 * 1024 * 1024
        ),
        cost_estimate=pl.CostEstimate(flops=4_000_000_000, bytes_accessed=9_000_000, transcendentals=0),
    )(tokens, jnp.transpose(in_weight, (1, 0, 2)), skip_gain.reshape(1, 128), response.reshape(2, 1024, 128),
      first, second, back, last, twist)


def solution(mesh):
    in_specs = (P("ctx", "tp"), P("tp", None, None), P("tp"), P(None, None, "ctx", "tp"))
    return jax.shard_map(
        per_device, mesh=mesh, in_specs=in_specs, out_specs=P("ctx", "tp"), check_vma=False
    )
```

profile of v0, /device:TPU:1, one launch (start us, length us, event | category | flops | bytes accessed | tf_op | source)
XLA Modules:
  0.0 61.1 jit_solution(1818195506104302525)
XLA Ops:
  0.0 0.0 copy-start
  0.0 1.2 %copy-done = bf16[512,1024]{1,0:T(8,128)(2,1)S(1)} copy-done((bf16[512,1024]{1,0:T(8,128)(2,1)S(1)}, bf16[512,1024]{1,0:T(8,128)(2,1)}, u32[]{:S(2)}) %copy-start) | copy-done | bytes 1048600
  1.2 0.0 copy-start.1
  1.2 1.2 %copy-done.1 = f32[2,512,2,128]{3,2,1,0:T(2,128)S(1)} copy-done((f32[2,512,2,128]{3,2,1,0:T(2,128)S(1)}, f32[2,512,2,128]{3,2,1,0:T(2,128)}, u32[]{:S(2)}) %copy-start.1) | copy-done | bytes 1048600
  2.5 0.0 copy-start.2
  2.5 0.7 %copy-done.2 = f32[128]{0:T(128)S(1)} copy-done((f32[128]{0:T(128)S(1)}, f32[128]{0:T(128)}, u32[]{:S(2)}) %copy-start.2) | copy-done | bytes 536
  3.1 0.0 copy-start.3
  3.1 0.9 %copy-done.3 = f32[2,256,128]{2,1,0:T(8,128)S(1)} copy-done((f32[2,256,128]{2,1,0:T(8,128)S(1)}, f32[2,256,128]{2,1,0:T(8,128)}, u32[]{:S(2)}) %copy-start.3) | copy-done | bytes 262168
  4.1 0.0 copy-start.4
  4.1 0.9 %copy-done.4 = bf16[128,512]{1,0:T(8,128)(2,1)S(1)} copy-done((bf16[128,512]{1,0:T(8,128)(2,1)S(1)}, bf16[128,512]{1,0:T(8,128)(2,1)}, u32[]{:S(2)}) %copy-start.4) | copy-done | bytes 131096
  5.0 0.0 copy-start.5
  5.0 0.9 %copy-done.5 = bf16[256,256]{1,0:T(8,128)(2,1)S(1)} copy-done((bf16[256,256]{1,0:T(8,128)(2,1)S(1)}, bf16[256,256]{1,0:T(8,128)(2,1)}, u32[]{:S(2)}) %copy-start.5) | copy-done | bytes 131096
  5.9 0.0 copy-start.6
  5.9 0.9 %copy-done.6 = bf16[256,256]{1,0:T(8,128)(2,1)S(1)} copy-done((bf16[256,256]{1,0:T(8,128)(2,1)S(1)}, bf16[256,256]{1,0:T(8,128)(2,1)}, u32[]{:S(2)}) %copy-start.6) | copy-done | bytes 131096
  6.8 0.0 copy-start.7
  6.8 0.9 %copy-done.7 = bf16[512,128]{1,0:T(8,128)(2,1)S(1)} copy-done((bf16[512,128]{1,0:T(8,128)(2,1)S(1)}, bf16[512,128]{1,0:T(8,128)(2,1)}, u32[]{:S(2)}) %copy-start.7) | copy-done | bytes 131096
  7.7 52.7 %shard_map.91 = bf16[512,128]{1,0:T(8,128)(2,1)S(1)} custom-call(bf16[512,1024]{1,0:T(8,128)(2,1)S(1)} %copy-done, bf16[3,1024,1024]{2,1,0:T(8,128)(2,1)} %bitcast.5, f32[1,128]{1,0:T(1,128)S(1)} %bitcast.4, f32[2,1024,128]{2,1,0:T(8,128)S(1)} %bitcast.3, bf16[512,128]{1,0:T(8,128)(2,1)S(1)} %copy-done.7, bf16[256,256]{1,0:T(8,128)(2,1)S(1)} %copy-done.6, ...), custom_call_target="tpu_custom_call" | custom-call | flops 4000000000 | bytes 9000000 | tf_op jit(solution)/shard_map/pallas_call | solution.py:263
  60.4 0.7 %copy.11 = bf16[512,128]{1,0:T(8,128)(2,1)} copy(bf16[512,128]{1,0:T(8,128)(2,1)S(1)} %shard_map.91) | data formatting | bytes 262144
Async XLA Ops:
  0.0 1.2 %copy-start = (bf16[512,1024]{1,0:T(8,128)(2,1)S(1)}, bf16[512,1024]{1,0:T(8,128)(2,1)}, u32[]{:S(2)}) copy-start(bf16[512,1024]{1,0:T(8,128)(2,1)} %tok_h.1) | copy-start | bytes 3145732
  1.2 1.2 %copy-start.1 = (f32[2,512,2,128]{3,2,1,0:T(2,128)S(1)}, f32[2,512,2,128]{3,2,1,0:T(2,128)}, u32[]{:S(2)}) copy-start(f32[2,512,2,128]{3,2,1,0:T(2,128)} %param.12) | copy-start | bytes 3145732
  2.5 0.7 %copy-start.2 = (f32[128]{0:T(128)S(1)}, f32[128]{0:T(128)}, u32[]{:S(2)}) copy-start(f32[128]{0:T(128)} %param.11) | copy-start | bytes 1540
  3.1 0.9 %copy-start.3 = (f32[2,256,128]{2,1,0:T(8,128)S(1)}, f32[2,256,128]{2,1,0:T(8,128)}, u32[]{:S(2)}) copy-start(f32[2,256,128]{2,1,0:T(8,128)} %constant.10.clone.tw_h) | copy-start | bytes 786436
  4.1 0.9 %copy-start.4 = (bf16[128,512]{1,0:T(8,128)(2,1)S(1)}, bf16[128,512]{1,0:T(8,128)(2,1)}, u32[]{:S(2)}) copy-start(bf16[128,512]{1,0:T(8,128)(2,1)} %constant.14.clone.g1_h) | copy-start | bytes 393220
  5.0 0.9 %copy-start.5 = (bf16[256,256]{1,0:T(8,128)(2,1)S(1)}, bf16[256,256]{1,0:T(8,128)(2,1)}, u32[]{:S(2)}) copy-start(bf16[256,256]{1,0:T(8,128)(2,1)} %constant.13.clone.g2_h) | copy-start | bytes 393220
  5.9 0.9 %copy-start.6 = (bf16[256,256]{1,0:T(8,128)(2,1)S(1)}, bf16[256,256]{1,0:T(8,128)(2,1)}, u32[]{:S(2)}) copy-start(bf16[256,256]{1,0:T(8,128)(2,1)} %constant.12.clone.f2_h) | copy-start | bytes 393220
  6.8 0.9 %copy-start.7 = (bf16[512,128]{1,0:T(8,128)(2,1)S(1)}, bf16[512,128]{1,0:T(8,128)(2,1)}, u32[]{:S(2)}) copy-start(bf16[512,128]{1,0:T(8,128)(2,1)} %constant.11.clone.f1_h) | copy-start | bytes 393220
where the time goes:
time: 62.1 us; the launch traced here: 61.1 us
  Pallas kernels  52.7 us (85%)
  local copies, waits for them, and re-layouts  8.33 us (13%)
    pallas_call x1, Pallas kernels, per_device(): pl.pallas_call(kernel, out_shape=jax.ShapeDtypeStruct((512, 128), BF16),...  52.7 us
    unnamed x17, local copies, waits for them, and re-layouts  8.33 us

commit v1 on v0

--- a/solution.py
+++ b/solution.py
@@ -48,11 +48,21 @@
     down = (me, zh * 4 + (y + 3) % 4)
     across = (me, (1 - zh) * 4 + y)
 
-    loads = [(tok_h, tok), (w_h.at[1], w.at[1]), (w_h.at[2], w.at[2]), (rsp_h, rsp), (w_h.at[0], w.at[0]),
-             (f1_h, f1), (f2_h, f2), (g2_h, g2), (g1_h, g1), (tw_h, tw)]
-    loads = [pltpu.make_async_copy(src, dst, load_sem.at[i]) for i, (src, dst) in enumerate(loads)]
+    def columns(z, dest_y):
+        return pl.ds(pl.multiple_of((z * 4 + dest_y) * 128, 128), 128)
+
+    far, near = 1 - zh, zh
+    pieces = [(rsp_h, rsp), (tok_h, tok), (w_h.at[1], w.at[1]), (w_h.at[2], w.at[2]), (w_h.at[0], w.at[0]),
+              (f1_h, f1), (f2_h, f2), (g2_h, g2), (g1_h, g1), (tw_h, tw)]
+    loads = [pltpu.make_async_copy(src, dst, load_sem.at[i]) for i, (src, dst) in enumerate(pieces)]
     for copy in loads:
         copy.start()
+    waited = []
+
+    def need(count):
+        while len(waited) < count:
+            loads[len(waited)].wait()
+            waited.append(True)
 
     barrier = pltpu.get_barrier_semaphore()
     for dev in (up, down, across):
@@ -65,15 +75,14 @@
     lax.fori_loop(1, 32, greet, 0)
 
     def term(u, dest_y):
+        if u >= 4:
+            value = jnp.dot(tok[...], w[0, :, columns((far, near)[u - 4], dest_y)], preferred_element_type=F32)
+            return jnp.concatenate([value[:256], value[256:]], axis=1)
         rows = pl.ds(u % 2 * 256, 256)
-        far = pl.ds(pl.multiple_of(((1 - zh) * 4 + dest_y) * 128, 128), 128)
-        near = pl.ds(pl.multiple_of((zh * 4 + dest_y) * 128, 128), 128)
         if u < 2:
-            rhs = [w[1, :, far], w[2, :, far]]
-        elif u < 4:
-            rhs = [w[1, :, near], w[2, :, near]]
+            rhs = [w[1, :, columns(far, dest_y)], w[2, :, columns(far, dest_y)]]
         else:
-            rhs = [w[0, :, far], w[0, :, near]]
+            rhs = [w[1, :, columns(near, dest_y)], w[2, :, columns(near, dest_y)]]
         return jnp.dot(tok[rows, :], jnp.concatenate(rhs, axis=1), preferred_element_type=F32)
 
     def remote(src, dst, ssem, rsem, dev):
@@ -92,9 +101,8 @@
                       rb_sem.at[u, 2 * side + half], (up, down)[side])
 
     def c_copy(u):
-        if u < 2:
-            return remote(sc.at[u], rc.at[u], sc_sem.at[u], rc_sem.at[u], across)
-        return remote(sc.at[u - 2, :, lo], rc.at[u - 2, :, lo], sc_sem.at[u - 2], rc_sem.at[u - 2], across)
+        slot = min(u, 2)
+        return remote(sc.at[slot], rc.at[slot], sc_sem.at[slot], rc_sem.at[slot], across)
 
     def compute_a(u):
         sa[u] = term(u, (y + 2) % 4).astype(BF16)
@@ -125,8 +133,8 @@
                 b_copy(u, side, half).wait_recv()
         total = own + rb[u, 0].astype(F32) + rb[u, 1].astype(F32)
         rows = pl.ds(u % 2 * 256, 256)
-        if u < 2:
-            sc[u] = total.astype(BF16)
+        if u in (0, 1, 4):
+            sc[min(u, 2)] = total.astype(BF16)
             c_copy(u).start()
         elif u < 4:
             c_copy(u - 2).wait_recv()
@@ -137,18 +145,21 @@
                 s = u % 2 * 2 + half
                 g32[pl.ds(s, 128, stride=4), :] = jnp.transpose(product[half * 128:half * 128 + 128, :])
         else:
-            sc[u - 2, :, lo] = total[:, :128].astype(BF16)
-            query[rows, :] = total[:, 128:]
-            c_copy(u).start()
-
-    def spread(src, dst, which):
+            c_copy(4).wait_recv()
+            total = total + rc[2].astype(F32)
+            query[pl.ds(0, 256), :] = total[:, :128]
+            query[pl.ds(256, 256), :] = total[:, 128:]
+
+    def spread(src, dst, which, first=1, last=32):
         def go(k, carry):
-            to = (me + k) % 32
+            to = (me // 8 + k // 8) % 4 * 8 + (me + k) % 8
             remote(src.at[to], dst.at[me], x_send.at[which], x_recv.at[which], (to, t)).start()
             return carry
 
-        lax.fori_loop(1, 32, go, 0)
-        dst[me] = src[me]
+        lax.fori_loop(max(first, 8), last, go, 0)
+        if first == 1:
+            lax.fori_loop(1, 8, go, 0)
+            dst[me] = src[me]
 
     def arrived(dst, which):
         others = dst.at[pl.ds(0, 31)]
@@ -158,51 +169,51 @@
         others = src.at[pl.ds(0, 31)]
         pltpu.make_async_copy(others, others, x_send.at[which]).wait()
 
-    for i in range(3):
-        loads[i].wait()
+    def ahead(u):
+        compute_a(u)
+        send_a(u)
+
+    def arrange_response():
+        need(1)
+        for ri in range(2):
+            for b in range(8):
+                hs32[pl.ds(ri * 8 + b, 128, stride=16), :] = jnp.transpose(rsp[ri, pl.ds(b, 128, stride=8), :])
+        hs[...] = hs32[...].astype(BF16).reshape(32, 64, 128)
+
+    def send_gated():
+        gs[...] = g32[...].astype(BF16).reshape(32, 16, 128)
+        spread(gs, gr, 1)
+
+    arrange_response()
+    need(4)
     compute_a(0)
     pl.semaphore_wait(barrier, 34)
     send_a(0)
     raw(0)
-    compute_a(1)
-    send_a(1)
-
-    loads[3].wait()
-    for ri in range(2):
-        for b in range(8):
-            hs32[pl.ds(ri * 8 + b, 128, stride=16), :] = jnp.transpose(rsp[ri, pl.ds(b, 128, stride=8), :])
-    hs[...] = hs32[...].astype(BF16).reshape(32, 64, 128)
     spread(hs, hr, 0)
-
+    ahead(1)
     add(0)
     raw(1)
-    compute_a(2)
-    send_a(2)
+    ahead(2)
     add(1)
+    raw(2)
     finish(0)
-    raw(2)
-    compute_a(3)
-    send_a(3)
+    ahead(3)
     add(2)
+    raw(3)
     finish(1)
-    raw(3)
-    loads[4].wait()
-    compute_a(4)
-    send_a(4)
+    need(10)
+    ahead(4)
     add(3)
+    raw(4)
+    ahead(5)
     finish(2)
-    raw(4)
-    finish(3)
-    gs[...] = g32[...].astype(BF16).reshape(32, 16, 128)
-    spread(gs, gr, 1)
-    compute_a(5)
-    send_a(5)
     add(4)
     raw(5)
+    finish(3)
+    send_gated()
     add(5)
     finish(4)
-    for i in range(5, 10):
-        loads[i].wait()
     arrived(hr, 0)
     arrived(gr, 1)
 
@@ -212,7 +223,7 @@
         axis=1).astype(BF16)
     mid = jnp.dot(f1[...], signal, preferred_element_type=F32)
     cosine, sine = tw[0], tw[1]
-    columns = []
+    waves = []
     for c in range(4):
         lanes = slice(c * 128, c * 128 + 128)
         re, im = mid[:256, lanes], mid[256:, lanes]
@@ -225,8 +236,8 @@
         filtered = jnp.concatenate([re * resp_re - im * resp_im, re * resp_im + im * resp_re], axis=1).astype(BF16)
         back = jnp.dot(filtered, g2[...], preferred_element_type=F32)
         re, im = back[:, :128], back[:, 128:]
-        columns.append(jnp.concatenate([re * cosine - im * sine, re * sine + im * cosine], axis=0).astype(BF16))
-    conv = jnp.dot(g1[...], jnp.concatenate(columns, axis=1), preferred_element_type=F32)
+        waves.append(jnp.concatenate([re * cosine - im * sine, re * sine + im * cosine], axis=0).astype(BF16))
+    conv = jnp.dot(g1[...], jnp.concatenate(waves, axis=1), preferred_element_type=F32)
     for c in range(4):
         for s in range(4):
             g32[pl.ds(c * 4 + s, 32, stride=16), :] = conv[s * 32:s * 32 + 32, c * 128:c * 128 + 128]
@@ -234,23 +245,20 @@
     spread(cs, cr, 2)
 
     finish(5)
-    for u in (4, 5):
-        c_copy(u).wait_recv()
     gain = skip_ref[...]
     arrived(cr, 2)
     g32[...] = cr[...].astype(F32).reshape(512, 128)
     for s in range(4):
         rows = pl.ds(s * 128, 128)
         conv_rows = jnp.transpose(g32[pl.ds(s, 128, stride=4), :])
-        q = query[rows, :] + rc[2 + s // 2, pl.ds(s % 2 * 128, 128), lo].astype(F32)
-        o_ref[rows, :] = (q * (conv_rows + gain * gat[rows, :])).astype(BF16)
+        o_ref[rows, :] = (query[rows, :] * (conv_rows + gain * gat[rows, :])).astype(BF16)
 
     for u in range(UNITS):
         for side in (0, 1):
             a_copy(u, side).wait_send()
             for half in (0, 1):
                 b_copy(u, side, half).wait_send()
-    for u in (0, 1, 4, 5):
+    for u in (0, 1, 4):
         c_copy(u).wait_send()
     for src, which in ((hs, 0), (gs, 1), (cs, 2)):
         left(src, which)
@@ -278,8 +286,8 @@
             pltpu.VMEM((UNITS, 256, 256), BF16),
             pltpu.VMEM((UNITS, 2, 256, 256), BF16),
             pltpu.VMEM((UNITS, 2, 256, 256), BF16),
-            pltpu.VMEM((4, 256, 256), BF16),
-            pltpu.VMEM((4, 256, 256), BF16),
+            pltpu.VMEM((3, 256, 256), BF16),
+            pltpu.VMEM((3, 256, 256), BF16),
             pltpu.VMEM((2, 2, 128, 256), F32),
             pltpu.VMEM((512, 128), F32),
             pltpu.VMEM((512, 128), F32),
@@ -296,13 +304,13 @@
             pltpu.SemaphoreType.DMA((UNITS, 2)),
             pltpu.SemaphoreType.DMA((UNITS, 4)),
             pltpu.SemaphoreType.DMA((UNITS, 4)),
-            pltpu.SemaphoreType.DMA((4,)),
-            pltpu.SemaphoreType.DMA((4,)),
+            pltpu.SemaphoreType.DMA((3,)),
+            pltpu.SemaphoreType.DMA((3,)),
             pltpu.SemaphoreType.DMA((3,)),
             pltpu.SemaphoreType.DMA((3,)),
         ],
         compiler_params=pltpu.CompilerParams(
-            collective_id=0, has_side_effects=True, vmem_limit_bytes=48 * 1024 * 1024
+            collective_id=0, has_side_effects=True, vmem_limit_bytes=60 * 1024 * 1024
         ),
         cost_estimate=pl.CostEstimate(flops=4_000_000_000, bytes_accessed=9_000_000, transcendentals=0),
     )(tokens, jnp.transpose(in_weight, (1, 0, 2)), skip_gain.reshape(1, 128), response.reshape(2, 1024, 128),

time: 62.1 us -> 55 us (0.89); the launches traced: 61.1 us -> 54.9 us
  local copies, waits for them, and re-layouts: 8.33 us -> 1.57 us
  Pallas kernels: 52.7 us -> 53.4 us
    unnamed x17 -> x1, local copies, waits for them, and re-layouts: 8.33 us -> 1.57 us
    pallas_call x1, Pallas kernels: 52.7 us -> 53.4 us  [per_device(): pl.pallas_call(kernel, out_shape=jax.ShapeDtypeStruct((512, 128), BF16),...]
where the time goes in v1:
time: 55 us; the launch traced here: 54.9 us
  Pallas kernels  53.4 us (97%)
  local copies, waits for them, and re-layouts  1.57 us (3%)
    pallas_call x1, Pallas kernels, per_device(): pl.pallas_call(kernel, out_shape=jax.ShapeDtypeStruct((512, 128), BF16),...  53.4 us
    unnamed x1, local copies, waits for them, and re-layouts  1.57 us

profile of v1, /device:TPU:1, one launch (start us, length us, event | category | flops | bytes accessed | tf_op | source)
XLA Modules:
  0.0 54.9 jit_solution(1479437842860432922)
XLA Ops:
  0.0 53.4 %shard_map.91 = bf16[512,128]{1,0:T(8,128)(2,1)} custom-call(bf16[512,1024]{1,0:T(8,128)(2,1)} %tok_h.1, bf16[3,1024,1024]{2,1,0:T(8,128)(2,1)} %bitcast.3, f32[1,128]{1,0:T(1,128)} %bitcast.5, f32[2,1024,128]{2,1,0:T(8,128)} %bitcast.4, bf16[512,128]{1,0:T(8,128)(2,1)} %constant.11.clone.f1_h, bf16[256,256]{1,0:T(8,128)(2,1)} %constant.12.clone.f2_h, ...), custom_call_target="tpu_custom_call" | custom-call | flops 4000000000 | bytes 9000000 | tf_op jit(solution)/shard_map/pallas_call | solution.py:271
  53.4 1.6 %copy.11 = bf16[512,128]{1,0:T(8,128)(2,1)} copy(bf16[512,128]{1,0:T(8,128)(2,1)} %shard_map.91) | data formatting | bytes 262144

commit v2 on v1

--- a/solution.py
+++ b/solution.py
@@ -189,25 +189,25 @@
     compute_a(0)
     pl.semaphore_wait(barrier, 34)
     send_a(0)
+    spread(hs, hr, 0)
     raw(0)
-    spread(hs, hr, 0)
     ahead(1)
     add(0)
     raw(1)
+    add(1)
     ahead(2)
-    add(1)
+    finish(0)
     raw(2)
-    finish(0)
+    finish(1)
+    add(2)
     ahead(3)
-    add(2)
     raw(3)
-    finish(1)
+    add(3)
     need(10)
     ahead(4)
-    add(3)
     raw(4)
+    finish(2)
     ahead(5)
-    finish(2)
     add(4)
     raw(5)
     finish(3)

time: 55 us -> 54.5 us (level)
  Pallas kernels: 53.4 us -> 52.7 us
    pallas_call x1, Pallas kernels: 53.4 us -> 52.7 us  [per_device(): pl.pallas_call(kernel, out_shape=jax.ShapeDtypeStruct((512, 128), BF16),...]
where the time goes in v2:
time: 54.5 us; the launch traced here: 54.3 us
  Pallas kernels  52.7 us (97%)
  local copies, waits for them, and re-layouts  1.57 us (3%)
    pallas_call x1, Pallas kernels, per_device(): pl.pallas_call(kernel, out_shape=jax.ShapeDtypeStruct((512, 128), BF16),...  52.7 us
    unnamed x1, local copies, waits for them, and re-layouts  1.57 us

profile of v2, /device:TPU:1, one launch (start us, length us, event | category | flops | bytes accessed | tf_op | source)
XLA Modules:
  0.0 54.3 jit_solution(13530657294906044358)
XLA Ops:
  0.0 52.7 %shard_map.91 = bf16[512,128]{1,0:T(8,128)(2,1)} custom-call(bf16[512,1024]{1,0:T(8,128)(2,1)} %tok_h.1, bf16[3,1024,1024]{2,1,0:T(8,128)(2,1)} %bitcast.3, f32[1,128]{1,0:T(1,128)} %bitcast.5, f32[2,1024,128]{2,1,0:T(8,128)} %bitcast.4, bf16[512,128]{1,0:T(8,128)(2,1)} %constant.11.clone.f1_h, bf16[256,256]{1,0:T(8,128)(2,1)} %constant.12.clone.f2_h, ...), custom_call_target="tpu_custom_call" | custom-call | flops 4000000000 | bytes 9000000 | tf_op jit(solution)/shard_map/pallas_call | solution.py:271
  52.7 1.6 %copy.11 = bf16[512,128]{1,0:T(8,128)(2,1)} copy(bf16[512,128]{1,0:T(8,128)(2,1)} %shard_map.91) | data formatting | bytes 262144

commit v3 on v2

--- a/solution.py
+++ b/solution.py
@@ -40,7 +40,7 @@
            tok, w, rsp, f1, f2, g2, g1, tw,
            sa, ra, sb, rb, sc, rc, part, gat, query,
            hs32, hs, hr, g32, gs, gr, cs, cr,
-           load_sem, sa_sem, ra_sem, sb_sem, rb_sem, sc_sem, rc_sem, x_send, x_recv):
+           load_sem, sa_sem, ra_sem, sb_sem, rb_sem, sc_sem, rc_sem, x_send, x_recv, z_ready):
     me = lax.axis_index("ctx")
     t = lax.axis_index("tp")
     zh, y = t // 4, t % 4
@@ -65,14 +65,30 @@
             waited.append(True)
 
     barrier = pltpu.get_barrier_semaphore()
-    for dev in (up, down, across):
+    for dev in (up, down):
         pl.semaphore_signal(barrier, inc=1, device_id=dev, device_id_type=MESH)
+
+    @pl.when(zh == 0)
+    def _():
+        pl.semaphore_signal(barrier, inc=1, device_id=across, device_id_type=MESH)
 
     def greet(k, carry):
         pl.semaphore_signal(barrier, inc=1, device_id=((me + k) % 32, t), device_id_type=MESH)
         return carry
 
     lax.fori_loop(1, 32, greet, 0)
+
+    def enter():
+        pl.semaphore_wait(barrier, 33 + zh)
+
+        @pl.when(zh == 1)
+        def _():
+            pl.semaphore_signal(z_ready, inc=1, device_id=across, device_id_type=MESH)
+
+    def across_present():
+        @pl.when(zh == 0)
+        def _():
+            pl.semaphore_wait(z_ready, 1)
 
     def term(u, dest_y):
         if u >= 4:
@@ -150,16 +166,15 @@
             query[pl.ds(0, 256), :] = total[:, :128]
             query[pl.ds(256, 256), :] = total[:, 128:]
 
-    def spread(src, dst, which, first=1, last=32):
+    def spread(src, dst, which):
         def go(k, carry):
             to = (me // 8 + k // 8) % 4 * 8 + (me + k) % 8
             remote(src.at[to], dst.at[me], x_send.at[which], x_recv.at[which], (to, t)).start()
             return carry
 
-        lax.fori_loop(max(first, 8), last, go, 0)
-        if first == 1:
-            lax.fori_loop(1, 8, go, 0)
-            dst[me] = src[me]
+        lax.fori_loop(8, 32, go, 0)
+        lax.fori_loop(1, 8, go, 0)
+        dst[me] = src[me]
 
     def arrived(dst, which):
         others = dst.at[pl.ds(0, 31)]
@@ -187,7 +202,7 @@
     arrange_response()
     need(4)
     compute_a(0)
-    pl.semaphore_wait(barrier, 34)
+    enter()
     send_a(0)
     spread(hs, hr, 0)
     raw(0)
@@ -196,6 +211,7 @@
     raw(1)
     add(1)
     ahead(2)
+    across_present()
     finish(0)
     raw(2)
     finish(1)
@@ -308,6 +324,7 @@
             pltpu.SemaphoreType.DMA((3,)),
             pltpu.SemaphoreType.DMA((3,)),
             pltpu.SemaphoreType.DMA((3,)),
+            pltpu.SemaphoreType.REGULAR,
         ],
         compiler_params=pltpu.CompilerParams(
             collective_id=0, has_side_effects=True, vmem_limit_bytes=60 * 1024 * 1024

time: 54.5 us -> 54.3 us (level); the launches traced: 54.3 us -> 53.5 us
  Pallas kernels: 52.7 us -> 51.9 us
    pallas_call x1, Pallas kernels: 52.7 us -> 51.9 us  [per_device(): pl.pallas_call(kernel, out_shape=jax.ShapeDtypeStruct((512, 128), BF16),...]
where the time goes in v3:
time: 54.3 us; the launch traced here: 53.5 us
  Pallas kernels  51.9 us (96%)
  local copies, waits for them, and re-layouts  1.57 us (3%)
    pallas_call x1, Pallas kernels, per_device(): pl.pallas_call(kernel, out_shape=jax.ShapeDtypeStruct((512, 128), BF16),...  51.9 us
    unnamed x1, local copies, waits for them, and re-layouts  1.57 us

profile of v3, /device:TPU:1, one launch (start us, length us, event | category | flops | bytes accessed | tf_op | source)
XLA Modules:
  0.0 53.5 jit_solution(15478632987318556162)
XLA Ops:
  0.0 51.9 %shard_map.91 = bf16[512,128]{1,0:T(8,128)(2,1)} custom-call(bf16[512,1024]{1,0:T(8,128)(2,1)} %tok_h.1, bf16[3,1024,1024]{2,1,0:T(8,128)(2,1)} %bitcast.3, f32[1,128]{1,0:T(1,128)} %bitcast.5, f32[2,1024,128]{2,1,0:T(8,128)} %bitcast.4, bf16[512,128]{1,0:T(8,128)(2,1)} %constant.11.clone.f1_h, bf16[256,256]{1,0:T(8,128)(2,1)} %constant.12.clone.f2_h, ...), custom_call_target="tpu_custom_call" | custom-call | flops 4000000000 | bytes 9000000 | tf_op jit(solution)/shard_map/pallas_call | solution.py:287
  51.9 1.6 %copy.11 = bf16[512,128]{1,0:T(8,128)(2,1)} copy(bf16[512,128]{1,0:T(8,128)(2,1)} %shard_map.91) | data formatting | bytes 262144

commit v4 on v3

--- a/solution.py
+++ b/solution.py
@@ -172,7 +172,9 @@
             remote(src.at[to], dst.at[me], x_send.at[which], x_recv.at[which], (to, t)).start()
             return carry
 
-        lax.fori_loop(8, 32, go, 0)
+        lax.fori_loop(16, 24, go, 0)
+        lax.fori_loop(8, 16, go, 0)
+        lax.fori_loop(24, 32, go, 0)
         lax.fori_loop(1, 8, go, 0)
         dst[me] = src[me]
 

time: 54.3 us -> 52.3 us (0.963); the launches traced: 53.5 us -> 52.2 us
  Pallas kernels: 51.9 us -> 50.6 us
    pallas_call x1, Pallas kernels: 51.9 us -> 50.6 us  [per_device(): pl.pallas_call(kernel, out_shape=jax.ShapeDtypeStruct((512, 128), BF16),...]
where the time goes in v4:
time: 52.3 us; the launch traced here: 52.2 us
  Pallas kernels  50.6 us (97%)
  local copies, waits for them, and re-layouts  1.57 us (3%)
    pallas_call x1, Pallas kernels, per_device(): pl.pallas_call(kernel, out_shape=jax.ShapeDtypeStruct((512, 128), BF16),...  50.6 us
    unnamed x1, local copies, waits for them, and re-layouts  1.57 us

profile of v4, /device:TPU:1, one launch (start us, length us, event | category | flops | bytes accessed | tf_op | source)
XLA Modules:
  0.0 52.2 jit_solution(3964566893595871611)
XLA Ops:
  0.0 50.6 %shard_map.91 = bf16[512,128]{1,0:T(8,128)(2,1)} custom-call(bf16[512,1024]{1,0:T(8,128)(2,1)} %tok_h.1, bf16[3,1024,1024]{2,1,0:T(8,128)(2,1)} %bitcast.3, f32[1,128]{1,0:T(1,128)} %bitcast.5, f32[2,1024,128]{2,1,0:T(8,128)} %bitcast.4, bf16[512,128]{1,0:T(8,128)(2,1)} %constant.11.clone.f1_h, bf16[256,256]{1,0:T(8,128)(2,1)} %constant.12.clone.f2_h, ...), custom_call_target="tpu_custom_call" | custom-call | flops 4000000000 | bytes 9000000 | tf_op jit(solution)/shard_map/pallas_call | solution.py:289
  50.6 1.6 %copy.11 = bf16[512,128]{1,0:T(8,128)(2,1)} copy(bf16[512,128]{1,0:T(8,128)(2,1)} %shard_map.91) | data formatting | bytes 262144
